TPU v7x, 128 devices: a whole 4x4x4 slice. The times are simulated.
128 devices in a mesh: gx: 16 (over z, y_hi, core), gy: 8 (over x, y_lo).
Axes of the slice: x: 4, y: 4 (y_hi: 2, y_lo: 2; y = y_hi * 2 + y_lo), z: 4, core: 2. Of those that a mesh axis runs over, the one named last changes fastest.
Arguments:
- state: float32 [4, 256, 128, 128], P(None, 'gx', 'gy'), may hold values from -4 to 4
- offsets: int32 [2], replicated, may hold values from 0 to 127
Outputs:
- advanced: float32 [4, 256, 128, 128], P(None, 'gx', 'gy')
All inputs are finite; a program needn't handle non-finite values.
Results may differ from a plain program's by a relative error of at most 0.00002.
Values sent between devices are 32-bit elements; how exact they have to be, the bound alone decides.
A program may use at most 64 MiB of HBM per device.

v0:
```python
import jax
import jax.numpy as jnp
from jax import lax
from jax.sharding import PartitionSpec as P

RELAX = 4
time_step = 0.2
viscosity = 0.1


def from_behind(value, axis, steps):
    count = lax.axis_size(axis)
    pairs = [(source, (source + steps) % count) for source in range(count)]
    return lax.ppermute(value, axis, pairs)


def extended(x, sides, width):
    for axis, dim in sides:
        size, length = (lax.axis_size(axis), x.shape[dim])
        up = [(i, (i + 1) % size) for i in range(size)]
        down = [(j, i) for i, j in up]
        last = lax.slice_in_dim(x, length - width, length, axis=dim)
        first = lax.slice_in_dim(x, 0, width, axis=dim)
        before = lax.ppermute(last, axis, up)
        after = lax.ppermute(first, axis, down)
        x = jnp.concatenate([before, x, after], axis=dim)
    return x


def shrink(ext):
    return ext[..., 1:-1, 1:-1, :]


def diff_x(ext):
    return (ext[..., 2:, 1:-1, :] - ext[..., :-2, 1:-1, :]) * 0.5


def diff_y(ext):
    return (ext[..., 1:-1, 2:, :] - ext[..., 1:-1, :-2, :]) * 0.5


def diff_z(center):
    return (jnp.roll(center, -1, -1) - jnp.roll(center, 1, -1)) * 0.5


def beside_all(ext):
    center = shrink(ext)
    total = ext[..., 2:, 1:-1, :] + ext[..., :-2, 1:-1, :]
    total = total + ext[..., 1:-1, 2:, :] + ext[..., 1:-1, :-2, :]
    return total + jnp.roll(center, -1, -1) + jnp.roll(center, 1, -1)


def move_rows(planes, amount):
    rows = planes.shape[2]
    span = rows * lax.axis_size("gy")
    whole = lax.all_gather(planes, "gy", axis=2, tiled=True)
    doubled = jnp.concatenate([whole, whole], axis=2)
    start = (lax.axis_index("gy") * rows + amount) % span
    return lax.dynamic_slice_in_dim(doubled, start, rows, 2)


def ghost(field, offset, width):
    lower = from_behind(field[:, -width:], "gx", 1)
    upper = from_behind(field[:, :width], "gx", -1)
    place = lax.axis_index("gx")
    count = lax.axis_size("gx")
    span = field.shape[2] * lax.axis_size("gy")
    amount = jnp.where(place == 0, -offset, offset) % span
    moved = move_rows(jnp.concatenate([lower, upper], axis=1), amount)
    left = jnp.where(place == 0, moved[:, :width], lower)
    right = jnp.where(place == count - 1, moved[:, width:], upper)
    grown = jnp.concatenate([left, field, right], axis=1)
    return extended(grown, (("gy", 2),), width)


def advance(state, offset, xpos, shear, half_width):
    mean_flow = (shear * (xpos + 0.5 - half_width))[:, None, None]
    ext = ghost(state, offset, 1)
    speed_x, speed_y, speed_z = (state[0], state[1], state[2])
    carried = speed_x * diff_x(ext) + (speed_y + mean_flow) * diff_y(ext) + speed_z * diff_z(state)
    tendency = viscosity * (beside_all(ext) - 6.0 * state) - carried
    zeros = jnp.zeros_like(speed_x)
    source = jnp.stack([zeros, -shear * speed_x, zeros, -speed_x])
    provisional = state + time_step * (tendency + source)
    velo = ghost(provisional[:3], offset, 1)
    rhs = (diff_x(velo[0]) + diff_y(velo[1]) + diff_z(provisional[2])) / time_step
    pressure = -rhs / 6.0
    for sweep in range(RELAX):
        padded = ghost(pressure[None], offset, 1)[0]
        pressure = (beside_all(padded) - rhs) / 6.0
    padded = ghost(pressure[None], offset, 1)[0]
    new_x = provisional[0] - time_step * diff_x(padded)
    new_y = provisional[1] - time_step * diff_y(padded)
    new_z = provisional[2] - time_step * diff_z(pressure)
    return jnp.stack([new_x, new_y, new_z, provisional[3]])


def local(state, offsets):
    slab = state.shape[1]
    total_x = slab * lax.axis_size("gx")
    shear = 2.0 / total_x
    half_width = total_x / 2.0
    xpos = (lax.axis_index("gx") * slab + jnp.arange(slab)).astype(jnp.float32)
    for step in range(offsets.shape[0]):
        state = advance(state, offsets[step], xpos, shear, half_width)
    return state


def solution(mesh):
    in_specs = (P(None, "gx", "gy", None), P())
    out_specs = P(None, "gx", "gy", None)
    return jax.shard_map(local, mesh=mesh, in_specs=in_specs, out_specs=out_specs, check_vma=False)
```

profile of v0, /device:TPU:14, one launch (start us, length us, event | category | flops | bytes accessed | tf_op | source)
XLA Modules:
  0.0 597.4 jit_solution(2945560103122616609)
XLA Ops:
  0.8 5.4 collective-permute-start.1
  10.6 29.0 %all_gather.42 = f32[4,2,128,128]{3,0,1,2:T(4,128)S(1)} all-gather(f32[4,2,16,128]{3,0,1,2:T(4,128)S(1)} %copy.551), channel_id=1, replica_groups=mesh['gx'=16,'gy'=8] {'gy'}, dimensions={2}, use_global_device_ids=true | all-gather | bytes 589824 | tf_op jit(solution)/shard_map/all_gather | solution.py:56
  40.0 4.2 collective-permute-start.3
  46.9 5.3 collective-permute-start.5
  53.8 28.7 %all_gather.43 = f32[3,2,128,128]{3,1,0,2:T(2,128)S(1)} all-gather(f32[3,2,16,128]{3,1,0,2:T(2,128)S(1)} %copy.558), channel_id=1, replica_groups=mesh['gx'=16,'gy'=8] {'gy'}, dimensions={2}, use_global_device_ids=true | all-gather | bytes 442368 | tf_op jit(solution)/shard_map/all_gather | solution.py:56
  82.7 4.1 collective-permute-start.6
  88.4 4.4 collective-permute-done.7
  93.1 5.3 collective-permute-start.9
  99.8 28.2 %all_gather.44 = f32[1,2,128,128]{3,1,0,2:T(2,128)S(1)} all-gather(f32[1,2,16,128]{3,1,0,2:T(2,128)S(1)} %copy.561), channel_id=1, replica_groups=mesh['gx'=16,'gy'=8] {'gy'}, dimensions={2}, use_global_device_ids=true | all-gather | bytes 147456 | tf_op jit(solution)/shard_map/all_gather | solution.py:56
  131.8 2.2 collective-permute-done.11
  134.5 5.3 collective-permute-start.13
  141.2 28.2 %all_gather.45 = f32[1,2,128,128]{3,1,0,2:T(2,128)S(1)} all-gather(f32[1,2,16,128]{3,1,0,2:T(2,128)S(1)} %copy.564), channel_id=1, replica_groups=mesh['gx'=16,'gy'=8] {'gy'}, dimensions={2}, use_global_device_ids=true | all-gather | bytes 147456 | tf_op jit(solution)/shard_map/all_gather | solution.py:56
  173.2 2.2 collective-permute-done.15
  175.9 5.3 collective-permute-start.17
  182.6 28.2 %all_gather.46 = f32[1,2,128,128]{3,1,0,2:T(2,128)S(1)} all-gather(f32[1,2,16,128]{3,1,0,2:T(2,128)S(1)} %copy.567), channel_id=1, replica_groups=mesh['gx'=16,'gy'=8] {'gy'}, dimensions={2}, use_global_device_ids=true | all-gather | bytes 147456 | tf_op jit(solution)/shard_map/all_gather | solution.py:56
  211.0 2.0 collective-permute-start.19
  214.6 2.2 collective-permute-done.19
  217.5 5.3 collective-permute-start.21
  224.2 28.2 %all_gather.47 = f32[1,2,128,128]{3,1,0,2:T(2,128)S(1)} all-gather(f32[1,2,16,128]{3,1,0,2:T(2,128)S(1)} %copy.570), channel_id=1, replica_groups=mesh['gx'=16,'gy'=8] {'gy'}, dimensions={2}, use_global_device_ids=true | all-gather | bytes 147456 | tf_op jit(solution)/shard_map/all_gather | solution.py:56
  256.2 2.2 collective-permute-done.23
  259.0 5.3 collective-permute-start.25
  265.7 28.2 %all_gather.48 = f32[1,2,128,128]{3,1,0,2:T(2,128)S(1)} all-gather(f32[1,2,16,128]{3,1,0,2:T(2,128)S(1)} %copy.573), channel_id=1, replica_groups=mesh['gx'=16,'gy'=8] {'gy'}, dimensions={2}, use_global_device_ids=true | all-gather | bytes 147456 | tf_op jit(solution)/shard_map/all_gather | solution.py:56
  294.0 2.0 collective-permute-start.27
  297.7 2.2 collective-permute-done.27
  300.4 5.3 collective-permute-start.29
  307.4 29.0 %all_gather.49 = f32[4,2,128,128]{3,0,1,2:T(4,128)S(1)} all-gather(f32[4,2,16,128]{3,0,1,2:T(4,128)S(1)} %copy.578), channel_id=1, replica_groups=mesh['gx'=16,'gy'=8] {'gy'}, dimensions={2}, use_global_device_ids=true | all-gather | bytes 589824 | tf_op jit(solution)/shard_map/all_gather | solution.py:56
  336.8 4.2 collective-permute-start.31
  343.6 5.3 collective-permute-start.33
  350.6 28.6 %all_gather.50 = f32[3,2,128,128]{3,1,0,2:T(2,128)S(1)} all-gather(f32[3,2,16,128]{3,1,0,2:T(2,128)S(1)} %copy.585), channel_id=1, replica_groups=mesh['gx'=16,'gy'=8] {'gy'}, dimensions={2}, use_global_device_ids=true | all-gather | bytes 442368 | tf_op jit(solution)/shard_map/all_gather | solution.py:56
  379.4 4.2 collective-permute-start.34
  385.1 4.4 collective-permute-done.35
  389.9 5.3 collective-permute-start.37
  396.6 28.2 %all_gather.51 = f32[1,2,128,128]{3,1,0,2:T(2,128)S(1)} all-gather(f32[1,2,16,128]{3,1,0,2:T(2,128)S(1)} %copy.588), channel_id=1, replica_groups=mesh['gx'=16,'gy'=8] {'gy'}, dimensions={2}, use_global_device_ids=true | all-gather | bytes 147456 | tf_op jit(solution)/shard_map/all_gather | solution.py:56
  424.9 2.0 collective-permute-start.39
  428.6 2.2 collective-permute-done.39
  431.3 5.3 collective-permute-start.41
  438.0 28.2 %all_gather.52 = f32[1,2,128,128]{3,1,0,2:T(2,128)S(1)} all-gather(f32[1,2,16,128]{3,1,0,2:T(2,128)S(1)} %copy.591), channel_id=1, replica_groups=mesh['gx'=16,'gy'=8] {'gy'}, dimensions={2}, use_global_device_ids=true | all-gather | bytes 147456 | tf_op jit(solution)/shard_map/all_gather | solution.py:56
  470.0 2.2 collective-permute-done.43
  472.7 5.3 collective-permute-start.45
  479.4 28.2 %all_gather.53 = f32[1,2,128,128]{3,1,0,2:T(2,128)S(1)} all-gather(f32[1,2,16,128]{3,1,0,2:T(2,128)S(1)} %copy.594), channel_id=1, replica_groups=mesh['gx'=16,'gy'=8] {'gy'}, dimensions={2}, use_global_device_ids=true | all-gather | bytes 147456 | tf_op jit(solution)/shard_map/all_gather | solution.py:56
  511.4 2.2 collective-permute-done.47
  514.1 5.3 collective-permute-start.49
  520.8 28.2 %all_gather.54 = f32[1,2,128,128]{3,1,0,2:T(2,128)S(1)} all-gather(f32[1,2,16,128]{3,1,0,2:T(2,128)S(1)} %copy.597), channel_id=1, replica_groups=mesh['gx'=16,'gy'=8] {'gy'}, dimensions={2}, use_global_device_ids=true | all-gather | bytes 147456 | tf_op jit(solution)/shard_map/all_gather | solution.py:56
  549.1 2.0 collective-permute-start.51
  552.8 2.2 collective-permute-done.51
  555.6 5.3 collective-permute-start.53
  562.3 28.2 %all_gather.55 = f32[1,2,128,128]{3,1,0,2:T(2,128)S(1)} all-gather(f32[1,2,16,128]{3,1,0,2:T(2,128)S(1)} %copy.600), channel_id=1, replica_groups=mesh['gx'=16,'gy'=8] {'gy'}, dimensions={2}, use_global_device_ids=true | all-gather | bytes 147456 | tf_op jit(solution)/shard_map/all_gather | solution.py:56
  594.3 2.2 collective-permute-done.55
  (255 shorter events, 66.0 us)
Async XLA Ops:
  0.8 9.8 %collective-permute-start = (f32[4,1,16,128]{3,2,1,0:T(8,128)S(1)}, f32[4,1,16,128]{3,2,1,0:T(8,128)S(1)}, u32[]{:S(2)}, u32[]{:S(2)}) collective-permute-start(f32[4,1,16,128]{3,2,1,0:T(8,128)S(1)} %get-tuple-element.39), channel_id=1, source_target_pairs={{0,8},{8,16},{16,24},{24,32},{32,40},{40,48},{48,56},{56,64},{64,7... | collective-permute-start | bytes 98312 | tf_op jit(solution)/shard_map/ppermute | solution.py:14
  0.8 9.8 %collective-permute-start.1 = (f32[4,1,16,128]{3,2,1,0:T(8,128)S(1)}, f32[4,1,16,128]{3,2,1,0:T(8,128)S(1)}, u32[]{:S(2)}, u32[]{:S(2)}) collective-permute-start(f32[4,1,16,128]{3,2,1,0:T(8,128)S(1)} %get-tuple-element.40), channel_id=1, source_target_pairs={{0,120},{8,0},{16,8},{24,16},{32,24},{40,32},{48,40},{56,48},{64,5... | collective-permute-start | bytes 98312 | tf_op jit(solution)/shard_map/ppermute | solution.py:14
  39.9 6.1 %collective-permute-start.2 = (f32[4,18,1,128]{3,0,2,1:T(4,128)S(1)}, f32[4,18,1,128]{3,0,2,1:T(4,128)S(1)}, u32[]{:S(2)}, u32[]{:S(2)}) collective-permute-start(f32[4,18,1,128]{3,0,2,1:T(4,128)S(1)} %copy.554), channel_id=1, source_target_pairs={{1,0},{2,1},{3,2},{4,3},{5,4},{6,5},{7,6},{0,7},{9,8},{10,9},{11,1... | collective-permute-start | bytes 110600 | tf_op jit(solution)/shard_map/ppermute | solution.py:25
  40.0 6.1 %collective-permute-start.3 = (f32[4,18,1,128]{3,0,2,1:T(4,128)S(1)}, f32[4,18,1,128]{3,0,2,1:T(4,128)S(1)}, u32[]{:S(2)}, u32[]{:S(2)}) collective-permute-start(f32[4,18,1,128]{3,0,2,1:T(4,128)S(1)} %copy.556), channel_id=1, source_target_pairs={{0,1},{1,2},{2,3},{3,4},{4,5},{5,6},{6,7},{7,0},{8,9},{9,10},{10,1... | collective-permute-start | bytes 110600 | tf_op jit(solution)/shard_map/ppermute | solution.py:24
  46.8 6.9 %collective-permute-start.4 = (f32[3,1,16,128]{3,2,1,0:T(8,128)S(1)}, f32[3,1,16,128]{3,2,1,0:T(8,128)S(1)}, u32[]{:S(2)}, u32[]{:S(2)}) collective-permute-start(f32[3,1,16,128]{3,2,1,0:T(8,128)S(1)} %get-tuple-element.32), channel_id=1, source_target_pairs={{0,8},{8,16},{16,24},{24,32},{32,40},{40,48},{48,56},{56,64},{64,7... | collective-permute-start | bytes 73736 | tf_op jit(solution)/shard_map/ppermute | solution.py:14
  46.9 6.9 %collective-permute-start.5 = (f32[3,1,16,128]{3,2,1,0:T(8,128)S(1)}, f32[3,1,16,128]{3,2,1,0:T(8,128)S(1)}, u32[]{:S(2)}, u32[]{:S(2)}) collective-permute-start(f32[3,1,16,128]{3,2,1,0:T(8,128)S(1)} %get-tuple-element.33), channel_id=1, source_target_pairs={{0,120},{8,0},{16,8},{24,16},{32,24},{40,32},{48,40},{56,48},{64,5... | collective-permute-start | bytes 73736 | tf_op jit(solution)/shard_map/ppermute | solution.py:14
  82.7 5.7 collective-permute-start.6
  86.8 6.0 collective-permute-start.7
  93.0 6.8 %collective-permute-start.8 = (f32[1,1,16,128]{3,2,1,0:T(8,128)S(1)}, f32[1,1,16,128]{3,2,1,0:T(8,128)S(1)}, u32[]{:S(2)}, u32[]{:S(2)}) collective-permute-start(f32[1,1,16,128]{3,2,1,0:T(8,128)S(1)} %get-tuple-element.137), channel_id=1, source_target_pairs={{0,8},{8,16},{16,24},{24,32},{32,40},{40,48},{48,56},{56,64},{64,7... | collective-permute-start | bytes 24584 | tf_op jit(solution)/shard_map/ppermute | solution.py:14
  93.1 6.7 %collective-permute-start.9 = (f32[1,1,16,128]{3,2,1,0:T(8,128)S(1)}, f32[1,1,16,128]{3,2,1,0:T(8,128)S(1)}, u32[]{:S(2)}, u32[]{:S(2)}) collective-permute-start(f32[1,1,16,128]{3,2,1,0:T(8,128)S(1)} %get-tuple-element.138), channel_id=1, source_target_pairs={{0,120},{8,0},{16,8},{24,16},{32,24},{40,32},{48,40},{56,48},{64,5... | collective-permute-start | bytes 24584 | tf_op jit(solution)/shard_map/ppermute | solution.py:14
  128.2 5.8 collective-permute-start.11
  134.4 6.8 %collective-permute-start.12 = (f32[1,1,16,128]{3,2,1,0:T(8,128)S(1)}, f32[1,1,16,128]{3,2,1,0:T(8,128)S(1)}, u32[]{:S(2)}, u32[]{:S(2)}) collective-permute-start(f32[1,1,16,128]{3,2,1,0:T(8,128)S(1)} %get-tuple-element.135), channel_id=1, source_target_pairs={{0,8},{8,16},{16,24},{24,32},{32,40},{40,48},{48,56},{56,64},{64,7... | collective-permute-start | bytes 24584 | tf_op jit(solution)/shard_map/ppermute | solution.py:14
  134.5 6.7 %collective-permute-start.13 = (f32[1,1,16,128]{3,2,1,0:T(8,128)S(1)}, f32[1,1,16,128]{3,2,1,0:T(8,128)S(1)}, u32[]{:S(2)}, u32[]{:S(2)}) collective-permute-start(f32[1,1,16,128]{3,2,1,0:T(8,128)S(1)} %get-tuple-element.136), channel_id=1, source_target_pairs={{0,120},{8,0},{16,8},{24,16},{32,24},{40,32},{48,40},{56,48},{64,5... | collective-permute-start | bytes 24584 | tf_op jit(solution)/shard_map/ppermute | solution.py:14
  169.5 3.7 collective-permute-start.14
  169.6 5.8 collective-permute-start.15
  175.8 6.8 %collective-permute-start.16 = (f32[1,1,16,128]{3,2,1,0:T(8,128)S(1)}, f32[1,1,16,128]{3,2,1,0:T(8,128)S(1)}, u32[]{:S(2)}, u32[]{:S(2)}) collective-permute-start(f32[1,1,16,128]{3,2,1,0:T(8,128)S(1)} %get-tuple-element.133), channel_id=1, source_target_pairs={{0,8},{8,16},{16,24},{24,32},{32,40},{40,48},{48,56},{56,64},{64,7... | collective-permute-start | bytes 24584 | tf_op jit(solution)/shard_map/ppermute | solution.py:14
  175.9 6.7 %collective-permute-start.17 = (f32[1,1,16,128]{3,2,1,0:T(8,128)S(1)}, f32[1,1,16,128]{3,2,1,0:T(8,128)S(1)}, u32[]{:S(2)}, u32[]{:S(2)}) collective-permute-start(f32[1,1,16,128]{3,2,1,0:T(8,128)S(1)} %get-tuple-element.134), channel_id=1, source_target_pairs={{0,120},{8,0},{16,8},{24,16},{32,24},{40,32},{48,40},{56,48},{64,5... | collective-permute-start | bytes 24584 | tf_op jit(solution)/shard_map/ppermute | solution.py:14
  211.0 5.8 collective-permute-start.19
  217.2 6.9 %collective-permute-start.20 = (f32[1,1,16,128]{3,2,1,0:T(8,128)S(1)}, f32[1,1,16,128]{3,2,1,0:T(8,128)S(1)}, u32[]{:S(2)}, u32[]{:S(2)}) collective-permute-start(f32[1,1,16,128]{3,2,1,0:T(8,128)S(1)} %get-tuple-element.131), channel_id=1, source_target_pairs={{0,8},{8,16},{16,24},{24,32},{32,40},{40,48},{48,56},{56,64},{64,7... | collective-permute-start | bytes 24584 | tf_op jit(solution)/shard_map/ppermute | solution.py:14
  217.5 6.7 %collective-permute-start.21 = (f32[1,1,16,128]{3,2,1,0:T(8,128)S(1)}, f32[1,1,16,128]{3,2,1,0:T(8,128)S(1)}, u32[]{:S(2)}, u32[]{:S(2)}) collective-permute-start(f32[1,1,16,128]{3,2,1,0:T(8,128)S(1)} %get-tuple-element.132), channel_id=1, source_target_pairs={{0,120},{8,0},{16,8},{24,16},{32,24},{40,32},{48,40},{56,48},{64,5... | collective-permute-start | bytes 24584 | tf_op jit(solution)/shard_map/ppermute | solution.py:14
  252.5 3.7 collective-permute-start.22
  252.5 5.8 collective-permute-start.23
  258.9 6.8 %collective-permute-start.24 = (f32[1,1,16,128]{3,2,1,0:T(8,128)S(1)}, f32[1,1,16,128]{3,2,1,0:T(8,128)S(1)}, u32[]{:S(2)}, u32[]{:S(2)}) collective-permute-start(f32[1,1,16,128]{3,2,1,0:T(8,128)S(1)} %get-tuple-element.129), channel_id=1, source_target_pairs={{0,8},{8,16},{16,24},{24,32},{32,40},{40,48},{48,56},{56,64},{64,7... | collective-permute-start | bytes 24584 | tf_op jit(solution)/shard_map/ppermute | solution.py:14
  259.0 6.7 %collective-permute-start.25 = (f32[1,1,16,128]{3,2,1,0:T(8,128)S(1)}, f32[1,1,16,128]{3,2,1,0:T(8,128)S(1)}, u32[]{:S(2)}, u32[]{:S(2)}) collective-permute-start(f32[1,1,16,128]{3,2,1,0:T(8,128)S(1)} %get-tuple-element.130), channel_id=1, source_target_pairs={{0,120},{8,0},{16,8},{24,16},{32,24},{40,32},{48,40},{56,48},{64,5... | collective-permute-start | bytes 24584 | tf_op jit(solution)/shard_map/ppermute | solution.py:14
  294.0 5.8 collective-permute-start.27
  300.3 7.0 %collective-permute-start.28 = (f32[4,1,16,128]{3,2,1,0:T(8,128)S(1)}, f32[4,1,16,128]{3,2,1,0:T(8,128)S(1)}, u32[]{:S(2)}, u32[]{:S(2)}) collective-permute-start(f32[4,1,16,128]{3,2,1,0:T(8,128)S(1)} %get-tuple-element.25), channel_id=1, source_target_pairs={{0,8},{8,16},{16,24},{24,32},{32,40},{40,48},{48,56},{56,64},{64,7... | collective-permute-start | bytes 98312 | tf_op jit(solution)/shard_map/ppermute | solution.py:14
  300.4 6.9 %collective-permute-start.29 = (f32[4,1,16,128]{3,2,1,0:T(8,128)S(1)}, f32[4,1,16,128]{3,2,1,0:T(8,128)S(1)}, u32[]{:S(2)}, u32[]{:S(2)}) collective-permute-start(f32[4,1,16,128]{3,2,1,0:T(8,128)S(1)} %get-tuple-element.26), channel_id=1, source_target_pairs={{0,120},{8,0},{16,8},{24,16},{32,24},{40,32},{48,40},{56,48},{64,5... | collective-permute-start | bytes 98312 | tf_op jit(solution)/shard_map/ppermute | solution.py:14
  336.7 6.1 %collective-permute-start.30 = (f32[4,18,1,128]{3,0,2,1:T(4,128)S(1)}, f32[4,18,1,128]{3,0,2,1:T(4,128)S(1)}, u32[]{:S(2)}, u32[]{:S(2)}) collective-permute-start(f32[4,18,1,128]{3,0,2,1:T(4,128)S(1)} %copy.581), channel_id=1, source_target_pairs={{1,0},{2,1},{3,2},{4,3},{5,4},{6,5},{7,6},{0,7},{9,8},{10,9},{11,1... | collective-permute-start | bytes 110600 | tf_op jit(solution)/shard_map/ppermute | solution.py:25
  336.8 6.1 %collective-permute-start.31 = (f32[4,18,1,128]{3,0,2,1:T(4,128)S(1)}, f32[4,18,1,128]{3,0,2,1:T(4,128)S(1)}, u32[]{:S(2)}, u32[]{:S(2)}) collective-permute-start(f32[4,18,1,128]{3,0,2,1:T(4,128)S(1)} %copy.583), channel_id=1, source_target_pairs={{0,1},{1,2},{2,3},{3,4},{4,5},{5,6},{6,7},{7,0},{8,9},{9,10},{10,1... | collective-permute-start | bytes 110600 | tf_op jit(solution)/shard_map/ppermute | solution.py:24
  343.6 6.9 %collective-permute-start.32 = (f32[3,1,16,128]{3,2,1,0:T(8,128)S(1)}, f32[3,1,16,128]{3,2,1,0:T(8,128)S(1)}, u32[]{:S(2)}, u32[]{:S(2)}) collective-permute-start(f32[3,1,16,128]{3,2,1,0:T(8,128)S(1)} %get-tuple-element.23), channel_id=1, source_target_pairs={{0,8},{8,16},{16,24},{24,32},{32,40},{40,48},{48,56},{56,64},{64,7... | collective-permute-start | bytes 73736 | tf_op jit(solution)/shard_map/ppermute | solution.py:14
  343.6 6.9 %collective-permute-start.33 = (f32[3,1,16,128]{3,2,1,0:T(8,128)S(1)}, f32[3,1,16,128]{3,2,1,0:T(8,128)S(1)}, u32[]{:S(2)}, u32[]{:S(2)}) collective-permute-start(f32[3,1,16,128]{3,2,1,0:T(8,128)S(1)} %get-tuple-element.24), channel_id=1, source_target_pairs={{0,120},{8,0},{16,8},{24,16},{32,24},{40,32},{48,40},{56,48},{64,5... | collective-permute-start | bytes 73736 | tf_op jit(solution)/shard_map/ppermute | solution.py:14
  379.4 5.8 collective-permute-start.34
  383.6 6.0 collective-permute-start.35
  389.8 6.8 %collective-permute-start.36 = (f32[1,1,16,128]{3,2,1,0:T(8,128)S(1)}, f32[1,1,16,128]{3,2,1,0:T(8,128)S(1)}, u32[]{:S(2)}, u32[]{:S(2)}) collective-permute-start(f32[1,1,16,128]{3,2,1,0:T(8,128)S(1)} %get-tuple-element.117), channel_id=1, source_target_pairs={{0,8},{8,16},{16,24},{24,32},{32,40},{40,48},{48,56},{56,64},{64,7... | collective-permute-start | bytes 24584 | tf_op jit(solution)/shard_map/ppermute | solution.py:14
  389.9 6.7 %collective-permute-start.37 = (f32[1,1,16,128]{3,2,1,0:T(8,128)S(1)}, f32[1,1,16,128]{3,2,1,0:T(8,128)S(1)}, u32[]{:S(2)}, u32[]{:S(2)}) collective-permute-start(f32[1,1,16,128]{3,2,1,0:T(8,128)S(1)} %get-tuple-element.118), channel_id=1, source_target_pairs={{0,120},{8,0},{16,8},{24,16},{32,24},{40,32},{48,40},{56,48},{64,5... | collective-permute-start | bytes 24584 | tf_op jit(solution)/shard_map/ppermute | solution.py:14
  424.9 5.8 collective-permute-start.39
  431.2 6.8 %collective-permute-start.40 = (f32[1,1,16,128]{3,2,1,0:T(8,128)S(1)}, f32[1,1,16,128]{3,2,1,0:T(8,128)S(1)}, u32[]{:S(2)}, u32[]{:S(2)}) collective-permute-start(f32[1,1,16,128]{3,2,1,0:T(8,128)S(1)} %get-tuple-element.115), channel_id=1, source_target_pairs={{0,8},{8,16},{16,24},{24,32},{32,40},{40,48},{48,56},{56,64},{64,7... | collective-permute-start | bytes 24584 | tf_op jit(solution)/shard_map/ppermute | solution.py:14
  431.3 6.7 %collective-permute-start.41 = (f32[1,1,16,128]{3,2,1,0:T(8,128)S(1)}, f32[1,1,16,128]{3,2,1,0:T(8,128)S(1)}, u32[]{:S(2)}, u32[]{:S(2)}) collective-permute-start(f32[1,1,16,128]{3,2,1,0:T(8,128)S(1)} %get-tuple-element.116), channel_id=1, source_target_pairs={{0,120},{8,0},{16,8},{24,16},{32,24},{40,32},{48,40},{56,48},{64,5... | collective-permute-start | bytes 24584 | tf_op jit(solution)/shard_map/ppermute | solution.py:14
  466.3 5.8 collective-permute-start.43
  472.6 6.8 %collective-permute-start.44 = (f32[1,1,16,128]{3,2,1,0:T(8,128)S(1)}, f32[1,1,16,128]{3,2,1,0:T(8,128)S(1)}, u32[]{:S(2)}, u32[]{:S(2)}) collective-permute-start(f32[1,1,16,128]{3,2,1,0:T(8,128)S(1)} %get-tuple-element.113), channel_id=1, source_target_pairs={{0,8},{8,16},{16,24},{24,32},{32,40},{40,48},{48,56},{56,64},{64,7... | collective-permute-start | bytes 24584 | tf_op jit(solution)/shard_map/ppermute | solution.py:14
  472.7 6.7 %collective-permute-start.45 = (f32[1,1,16,128]{3,2,1,0:T(8,128)S(1)}, f32[1,1,16,128]{3,2,1,0:T(8,128)S(1)}, u32[]{:S(2)}, u32[]{:S(2)}) collective-permute-start(f32[1,1,16,128]{3,2,1,0:T(8,128)S(1)} %get-tuple-element.114), channel_id=1, source_target_pairs={{0,120},{8,0},{16,8},{24,16},{32,24},{40,32},{48,40},{56,48},{64,5... | collective-permute-start | bytes 24584 | tf_op jit(solution)/shard_map/ppermute | solution.py:14
  507.7 5.8 collective-permute-start.47
  514.0 6.8 %collective-permute-start.48 = (f32[1,1,16,128]{3,2,1,0:T(8,128)S(1)}, f32[1,1,16,128]{3,2,1,0:T(8,128)S(1)}, u32[]{:S(2)}, u32[]{:S(2)}) collective-permute-start(f32[1,1,16,128]{3,2,1,0:T(8,128)S(1)} %get-tuple-element.111), channel_id=1, source_target_pairs={{0,8},{8,16},{16,24},{24,32},{32,40},{40,48},{48,56},{56,64},{64,7... | collective-permute-start | bytes 24584 | tf_op jit(solution)/shard_map/ppermute | solution.py:14
  514.1 6.7 %collective-permute-start.49 = (f32[1,1,16,128]{3,2,1,0:T(8,128)S(1)}, f32[1,1,16,128]{3,2,1,0:T(8,128)S(1)}, u32[]{:S(2)}, u32[]{:S(2)}) collective-permute-start(f32[1,1,16,128]{3,2,1,0:T(8,128)S(1)} %get-tuple-element.112), channel_id=1, source_target_pairs={{0,120},{8,0},{16,8},{24,16},{32,24},{40,32},{48,40},{56,48},{64,5... | collective-permute-start | bytes 24584 | tf_op jit(solution)/shard_map/ppermute | solution.py:14
  549.1 5.8 collective-permute-start.51
  555.5 6.8 %collective-permute-start.52 = (f32[1,1,16,128]{3,2,1,0:T(8,128)S(1)}, f32[1,1,16,128]{3,2,1,0:T(8,128)S(1)}, u32[]{:S(2)}, u32[]{:S(2)}) collective-permute-start(f32[1,1,16,128]{3,2,1,0:T(8,128)S(1)} %get-tuple-element.105), channel_id=1, source_target_pairs={{0,8},{8,16},{16,24},{24,32},{32,40},{40,48},{48,56},{56,64},{64,7... | collective-permute-start | bytes 24584 | tf_op jit(solution)/shard_map/ppermute | solution.py:14
  555.6 6.7 %collective-permute-start.53 = (f32[1,1,16,128]{3,2,1,0:T(8,128)S(1)}, f32[1,1,16,128]{3,2,1,0:T(8,128)S(1)}, u32[]{:S(2)}, u32[]{:S(2)}) collective-permute-start(f32[1,1,16,128]{3,2,1,0:T(8,128)S(1)} %get-tuple-element.106), channel_id=1, source_target_pairs={{0,120},{8,0},{16,8},{24,16},{32,24},{40,32},{48,40},{56,48},{64,5... | collective-permute-start | bytes 24584 | tf_op jit(solution)/shard_map/ppermute | solution.py:14
  590.6 5.8 collective-permute-start.55
  (10 other events, 32.0 us)
where the time goes:
time: 598 us; the launch traced here: 597 us
  blocking collectives  397 us (66%)
  starting transfers between devices  114 us (19%)
  waiting for transfers between devices  69.7 us (12%)
  local copies, waits for them, and re-layouts  7.44 us (1%)
    all_gather x14, blocking collectives, move_rows(): whole = lax.all_gather(planes, 'gy', axis=2, tiled=True)  397 us
    ppermute x28, starting transfers between devices, from_behind(): return lax.ppermute(value, axis, pairs)  76 us
    ppermute x14, waiting for transfers between devices, extended(): after = lax.ppermute(first, axis, down)  34.4 us
    ppermute x14, starting transfers between devices, extended(): after = lax.ppermute(first, axis, down)  20.2 us
    ppermute x28, waiting for transfers between devices, from_behind(): return lax.ppermute(value, axis, pairs)  17.7 us
    ppermute x14, starting transfers between devices, extended(): before = lax.ppermute(last, axis, up)  17.7 us
    ppermute x14, waiting for transfers between devices, extended(): before = lax.ppermute(last, axis, up)  17.6 us
  transfers between devices with their start and end apart: 56, of which 40 were waited for; matrix products, arithmetic and copies ran while one was open for 1% of the time, Pallas kernels for 0%

commit v1 on v0

--- a/solution.py
+++ b/solution.py
@@ -2,6 +2,7 @@
 import jax.numpy as jnp
 from jax import lax
 from jax.sharding import PartitionSpec as P
+from jax.lax import all_to_all, axis_size
 
 RELAX = 4
 time_step = 0.2
@@ -53,7 +54,15 @@
 def move_rows(planes, amount):
     rows = planes.shape[2]
     span = rows * lax.axis_size("gy")
-    whole = lax.all_gather(planes, "gy", axis=2, tiled=True)
+    whole = jnp.concatenate(
+        all_to_all(
+            jnp.stack([planes for _ in range(axis_size("gy"))], axis=0),
+            axis_name="gy",
+            split_axis=0,
+            concat_axis=0,
+        ),
+        axis=2,
+    )
     doubled = jnp.concatenate([whole, whole], axis=2)
     start = (lax.axis_index("gy") * rows + amount) % span
     return lax.dynamic_slice_in_dim(doubled, start, rows, 2)

time: 598 us -> 368 us (0.62)
  blocking collectives: 397 us -> 72.9 us
  waiting for transfers between devices: 69.7 us -> 120 us
  starting transfers between devices: 114 us -> 152 us
    all_gather x14 -> x0, blocking collectives: 397 us -> none  [move_rows(): whole = lax.all_gather(planes, 'gy', axis=2, tiled=True)]
    all_to_all x0 -> x8, blocking collectives: none -> 72.9 us  [move_rows(): all_to_all(jnp.stack([planes for _ in range(axis_size('gy'))], axis=0), a...]
    all_to_all x0 -> x6, starting transfers between devices: none -> 37.2 us  [move_rows(): all_to_all(jnp.stack([planes for _ in range(axis_size('gy'))], axis=0), a...]
    all_to_all x0 -> x6, waiting for transfers between devices: none -> 30.3 us  [move_rows(): all_to_all(jnp.stack([planes for _ in range(axis_size('gy'))], axis=0), a...]
    ppermute x14, waiting for transfers between devices: 34.4 us -> 56.4 us  [extended(): after = lax.ppermute(first, axis, down)]
    ppermute x14, starting transfers between devices: 17.7 us -> 37 us  [extended(): before = lax.ppermute(last, axis, up)]
    ppermute x14, starting transfers between devices: 20.2 us -> 1.94 us  [extended(): after = lax.ppermute(first, axis, down)]
  transfers between devices with their start and end apart: 56 -> 62, of which waited for: 40 -> 45; matrix products, arithmetic and copies ran while one was open for 1% -> 1% of each run, Pallas kernels for 0% -> 0%
where the time goes in v1:
time: 368 us; the launch traced here: 367 us
  starting transfers between devices  152 us (41%)
  waiting for transfers between devices  120 us (33%)
  blocking collectives  72.9 us (20%)
  local copies, waits for them, and re-layouts  12.4 us (3%)
  other arithmetic  6.15 us (2%)
    ppermute x28, starting transfers between devices, from_behind(): return lax.ppermute(value, axis, pairs)  75.8 us
    all_to_all x8, blocking collectives, move_rows(): all_to_all(jnp.stack([planes for _ in range(axis_size('gy'))], axis=0), a...  72.9 us
    ppermute x14, waiting for transfers between devices, extended(): after = lax.ppermute(first, axis, down)  56.4 us
    all_to_all x6, starting transfers between devices, move_rows(): all_to_all(jnp.stack([planes for _ in range(axis_size('gy'))], axis=0), a...  37.2 us
    ppermute x14, starting transfers between devices, extended(): before = lax.ppermute(last, axis, up)  37 us
    all_to_all x6, waiting for transfers between devices, move_rows(): all_to_all(jnp.stack([planes for _ in range(axis_size('gy'))], axis=0), a...  30.3 us
    ppermute x28, waiting for transfers between devices, from_behind(): return lax.ppermute(value, axis, pairs)  16.8 us
    ppermute x14, waiting for transfers between devices, extended(): before = lax.ppermute(last, axis, up)  16.5 us
  transfers between devices with their start and end apart: 62, of which 45 were waited for; matrix products, arithmetic and copies ran while one was open for 1% of the time, Pallas kernels for 0%

profile of v1, /device:TPU:14, one launch (start us, length us, event | category | flops | bytes accessed | tf_op | source)
XLA Modules:
  0.0 367.1 jit_solution(13462691082775376220)
XLA Ops:
  0.8 5.4 %collective-permute-start.1 = (f32[4,1,16,128]{3,2,1,0:T(8,128)S(1)}, f32[4,1,16,128]{3,2,1,0:T(8,128)S(1)}, u32[]{:S(2)}, u32[]{:S(2)}) collective-permute-start(f32[4,1,16,128]{3,2,1,0:T(8,128)S(1)} %get-tuple-element.40), channel_id=1, source_target_pairs={{0,120},{8,0},{16,8},{24,16},{32,24},{40,32},{48,40},{56,48},{64,5... | collective-permute-start | bytes 98312 | tf_op jit(solution)/shard_map/ppermute | solution.py:15
  9.6 5.8 %all-to-all-start = ((f32[8,4,2,16,128]{4,3,2,1,0:T(8,128)}), f32[8,4,2,16,128]{4,3,2,1,0:T(8,128)S(1)}, u32[]{:S(2)}, u32[]{:S(2)}) async-start(f32[8,4,2,16,128]{4,3,2,1,0:T(8,128)} %stack.48), calls=%async_computation | async-start | bytes 1048576 | tf_op jit(solution)/shard_map/all_to_all | solution.py:58
  15.8 6.5 %all-to-all-done = f32[8,4,2,16,128]{4,3,2,1,0:T(8,128)S(1)} async-done(((f32[8,4,2,16,128]{4,3,2,1,0:T(8,128)}), f32[8,4,2,16,128]{4,3,2,1,0:T(8,128)S(1)}, u32[]{:S(2)}, u32[]{:S(2)}) %all-to-all-start) | async-done | bytes 524320 | tf_op jit(solution)/shard_map/all_to_all | solution.py:58
  23.1 3.6 collective-permute-start.3
  29.4 5.3 %collective-permute-start.5 = (f32[3,1,16,128]{3,2,1,0:T(8,128)S(1)}, f32[3,1,16,128]{3,2,1,0:T(8,128)S(1)}, u32[]{:S(2)}, u32[]{:S(2)}) collective-permute-start(f32[3,1,16,128]{3,2,1,0:T(8,128)S(1)} %get-tuple-element.33), channel_id=1, source_target_pairs={{0,120},{8,0},{16,8},{24,16},{32,24},{40,32},{48,40},{56,48},{64,5... | collective-permute-start | bytes 73736 | tf_op jit(solution)/shard_map/ppermute | solution.py:15
  37.0 7.5 %all-to-all-start.1 = ((f32[8,3,2,16,128]{4,3,2,1,0:T(8,128)}), f32[8,3,2,16,128]{4,3,2,1,0:T(8,128)S(1)}, u32[]{:S(2)}, u32[]{:S(2)}) async-start(f32[8,3,2,16,128]{4,3,2,1,0:T(8,128)} %stack.50), calls=%async_computation.1 | async-start | bytes 786432 | tf_op jit(solution)/shard_map/all_to_all | solution.py:58
  44.7 6.3 %all-to-all-done.1 = f32[8,3,2,16,128]{4,3,2,1,0:T(8,128)S(1)} async-done(((f32[8,3,2,16,128]{4,3,2,1,0:T(8,128)}), f32[8,3,2,16,128]{4,3,2,1,0:T(8,128)S(1)}, u32[]{:S(2)}, u32[]{:S(2)}) %all-to-all-start.1) | async-done | bytes 393248 | tf_op jit(solution)/shard_map/all_to_all | solution.py:58
  55.0 4.3 %collective-permute-done.7 = f32[3,18,1,128]{3,2,1,0:T(1,128)S(1)} collective-permute-done((f32[3,18,1,128]{3,2,1,0:T(1,128)S(1)}, f32[3,18,1,128]{3,2,1,0:T(1,128)S(1)}, u32[]{:S(2)}, u32[]{:S(2)}) %collective-permute-start.7) | collective-permute-done | bytes 27680 | tf_op jit(solution)/shard_map/ppermute | solution.py:26
  59.6 5.3 %collective-permute-start.9 = (f32[1,1,16,128]{3,2,1,0:T(8,128)S(1)}, f32[1,1,16,128]{3,2,1,0:T(8,128)S(1)}, u32[]{:S(2)}, u32[]{:S(2)}) collective-permute-start(f32[1,1,16,128]{3,2,1,0:T(8,128)S(1)} %get-tuple-element.138), channel_id=1, source_target_pairs={{0,120},{8,0},{16,8},{24,16},{32,24},{40,32},{48,40},{56,48},{64,5... | collective-permute-start | bytes 24584 | tf_op jit(solution)/shard_map/ppermute | solution.py:15
  66.4 9.1 %all_to_all.70 = f32[8,1,2,16,128]{4,3,2,1,0:T(8,128)S(1)} all-to-all(f32[8,1,2,16,128]{4,3,2,1,0:T(8,128)S(1)} %stack.51), channel_id=1, replica_groups=mesh['gx'=16,'gy'=8] {'gy'}, dimensions={0} | all-to-all | bytes 262144 | tf_op jit(solution)/shard_map/all_to_all | solution.py:58
  79.5 4.4 %collective-permute-done.11 = f32[1,18,1,128]{3,2,1,0:T(1,128)S(1)} collective-permute-done((f32[1,18,1,128]{3,2,1,0:T(1,128)S(1)}, f32[1,18,1,128]{3,2,1,0:T(1,128)S(1)}, u32[]{:S(2)}, u32[]{:S(2)}) %collective-permute-start.11) | collective-permute-done | bytes 9248 | tf_op jit(solution)/shard_map/ppermute | solution.py:26
  84.4 5.3 %collective-permute-start.13 = (f32[1,1,16,128]{3,2,1,0:T(8,128)S(1)}, f32[1,1,16,128]{3,2,1,0:T(8,128)S(1)}, u32[]{:S(2)}, u32[]{:S(2)}) collective-permute-start(f32[1,1,16,128]{3,2,1,0:T(8,128)S(1)} %get-tuple-element.136), channel_id=1, source_target_pairs={{0,120},{8,0},{16,8},{24,16},{32,24},{40,32},{48,40},{56,48},{64,5... | collective-permute-start | bytes 24584 | tf_op jit(solution)/shard_map/ppermute | solution.py:15
  91.1 9.1 %all_to_all.71 = f32[8,1,2,16,128]{4,3,2,1,0:T(8,128)S(1)} all-to-all(f32[8,1,2,16,128]{4,3,2,1,0:T(8,128)S(1)} %stack.52), channel_id=1, replica_groups=mesh['gx'=16,'gy'=8] {'gy'}, dimensions={0} | all-to-all | bytes 262144 | tf_op jit(solution)/shard_map/all_to_all | solution.py:58
  104.3 4.4 %collective-permute-done.15 = f32[1,18,1,128]{3,2,1,0:T(1,128)S(1)} collective-permute-done((f32[1,18,1,128]{3,2,1,0:T(1,128)S(1)}, f32[1,18,1,128]{3,2,1,0:T(1,128)S(1)}, u32[]{:S(2)}, u32[]{:S(2)}) %collective-permute-start.15) | collective-permute-done | bytes 9248 | tf_op jit(solution)/shard_map/ppermute | solution.py:26
  109.2 5.3 %collective-permute-start.17 = (f32[1,1,16,128]{3,2,1,0:T(8,128)S(1)}, f32[1,1,16,128]{3,2,1,0:T(8,128)S(1)}, u32[]{:S(2)}, u32[]{:S(2)}) collective-permute-start(f32[1,1,16,128]{3,2,1,0:T(8,128)S(1)} %get-tuple-element.134), channel_id=1, source_target_pairs={{0,120},{8,0},{16,8},{24,16},{32,24},{40,32},{48,40},{56,48},{64,5... | collective-permute-start | bytes 24584 | tf_op jit(solution)/shard_map/ppermute | solution.py:15
  115.9 9.1 %all_to_all.72 = f32[8,1,2,16,128]{4,3,2,1,0:T(8,128)S(1)} all-to-all(f32[8,1,2,16,128]{4,3,2,1,0:T(8,128)S(1)} %stack.53), channel_id=1, replica_groups=mesh['gx'=16,'gy'=8] {'gy'}, dimensions={0} | all-to-all | bytes 262144 | tf_op jit(solution)/shard_map/all_to_all | solution.py:58
  129.0 4.4 %collective-permute-done.19 = f32[1,18,1,128]{3,2,1,0:T(1,128)S(1)} collective-permute-done((f32[1,18,1,128]{3,2,1,0:T(1,128)S(1)}, f32[1,18,1,128]{3,2,1,0:T(1,128)S(1)}, u32[]{:S(2)}, u32[]{:S(2)}) %collective-permute-start.19) | collective-permute-done | bytes 9248 | tf_op jit(solution)/shard_map/ppermute | solution.py:26
  133.9 5.3 %collective-permute-start.21 = (f32[1,1,16,128]{3,2,1,0:T(8,128)S(1)}, f32[1,1,16,128]{3,2,1,0:T(8,128)S(1)}, u32[]{:S(2)}, u32[]{:S(2)}) collective-permute-start(f32[1,1,16,128]{3,2,1,0:T(8,128)S(1)} %get-tuple-element.132), channel_id=1, source_target_pairs={{0,120},{8,0},{16,8},{24,16},{32,24},{40,32},{48,40},{56,48},{64,5... | collective-permute-start | bytes 24584 | tf_op jit(solution)/shard_map/ppermute | solution.py:15
  140.7 9.1 %all_to_all.73 = f32[8,1,2,16,128]{4,3,2,1,0:T(8,128)S(1)} all-to-all(f32[8,1,2,16,128]{4,3,2,1,0:T(8,128)S(1)} %stack.54), channel_id=1, replica_groups=mesh['gx'=16,'gy'=8] {'gy'}, dimensions={0} | all-to-all | bytes 262144 | tf_op jit(solution)/shard_map/all_to_all | solution.py:58
  153.8 4.4 %collective-permute-done.23 = f32[1,18,1,128]{3,2,1,0:T(1,128)S(1)} collective-permute-done((f32[1,18,1,128]{3,2,1,0:T(1,128)S(1)}, f32[1,18,1,128]{3,2,1,0:T(1,128)S(1)}, u32[]{:S(2)}, u32[]{:S(2)}) %collective-permute-start.23) | collective-permute-done | bytes 9248 | tf_op jit(solution)/shard_map/ppermute | solution.py:26
  158.7 5.3 %collective-permute-start.25 = (f32[1,1,16,128]{3,2,1,0:T(8,128)S(1)}, f32[1,1,16,128]{3,2,1,0:T(8,128)S(1)}, u32[]{:S(2)}, u32[]{:S(2)}) collective-permute-start(f32[1,1,16,128]{3,2,1,0:T(8,128)S(1)} %get-tuple-element.130), channel_id=1, source_target_pairs={{0,120},{8,0},{16,8},{24,16},{32,24},{40,32},{48,40},{56,48},{64,5... | collective-permute-start | bytes 24584 | tf_op jit(solution)/shard_map/ppermute | solution.py:15
  166.1 5.4 %all-to-all-start.6 = ((f32[8,1,2,16,128]{4,3,2,1,0:T(8,128)}), f32[8,1,2,16,128]{4,3,2,1,0:T(8,128)S(1)}, u32[]{:S(2)}, u32[]{:S(2)}) async-start(f32[8,1,2,16,128]{4,3,2,1,0:T(8,128)} %stack.55), calls=%async_computation.6 | async-start | bytes 262144 | tf_op jit(solution)/shard_map/all_to_all | solution.py:58
  171.6 3.8 %all-to-all-done.6 = f32[8,1,2,16,128]{4,3,2,1,0:T(8,128)S(1)} async-done(((f32[8,1,2,16,128]{4,3,2,1,0:T(8,128)}), f32[8,1,2,16,128]{4,3,2,1,0:T(8,128)S(1)}, u32[]{:S(2)}, u32[]{:S(2)}) %all-to-all-start.6) | async-done | bytes 131104 | tf_op jit(solution)/shard_map/all_to_all | solution.py:58
  179.4 4.4 %collective-permute-done.27 = f32[1,18,1,128]{3,2,1,0:T(1,128)S(1)} collective-permute-done((f32[1,18,1,128]{3,2,1,0:T(1,128)S(1)}, f32[1,18,1,128]{3,2,1,0:T(1,128)S(1)}, u32[]{:S(2)}, u32[]{:S(2)}) %collective-permute-start.27) | collective-permute-done | bytes 9248 | tf_op jit(solution)/shard_map/ppermute | solution.py:26
  184.8 5.3 %collective-permute-start.29 = (f32[4,1,16,128]{3,2,1,0:T(8,128)S(1)}, f32[4,1,16,128]{3,2,1,0:T(8,128)S(1)}, u32[]{:S(2)}, u32[]{:S(2)}) collective-permute-start(f32[4,1,16,128]{3,2,1,0:T(8,128)S(1)} %get-tuple-element.26), channel_id=1, source_target_pairs={{0,120},{8,0},{16,8},{24,16},{32,24},{40,32},{48,40},{56,48},{64,5... | collective-permute-start | bytes 98312 | tf_op jit(solution)/shard_map/ppermute | solution.py:15
  193.2 5.4 %all-to-all-start.7 = ((f32[8,4,2,16,128]{4,3,2,1,0:T(8,128)}), f32[8,4,2,16,128]{4,3,2,1,0:T(8,128)S(1)}, u32[]{:S(2)}, u32[]{:S(2)}) async-start(f32[8,4,2,16,128]{4,3,2,1,0:T(8,128)} %stack.59), calls=%async_computation.7 | async-start | bytes 1048576 | tf_op jit(solution)/shard_map/all_to_all | solution.py:58
  199.8 4.8 %all-to-all-done.7 = f32[8,4,2,16,128]{4,3,2,1,0:T(8,128)S(1)} async-done(((f32[8,4,2,16,128]{4,3,2,1,0:T(8,128)}), f32[8,4,2,16,128]{4,3,2,1,0:T(8,128)S(1)}, u32[]{:S(2)}, u32[]{:S(2)}) %all-to-all-start.7) | async-done | bytes 524320 | tf_op jit(solution)/shard_map/all_to_all | solution.py:58
  206.8 2.9 collective-permute-start.31
  212.4 5.3 %collective-permute-start.33 = (f32[3,1,16,128]{3,2,1,0:T(8,128)S(1)}, f32[3,1,16,128]{3,2,1,0:T(8,128)S(1)}, u32[]{:S(2)}, u32[]{:S(2)}) collective-permute-start(f32[3,1,16,128]{3,2,1,0:T(8,128)S(1)} %get-tuple-element.24), channel_id=1, source_target_pairs={{0,120},{8,0},{16,8},{24,16},{32,24},{40,32},{48,40},{56,48},{64,5... | collective-permute-start | bytes 73736 | tf_op jit(solution)/shard_map/ppermute | solution.py:15
  220.1 7.6 %all-to-all-start.8 = ((f32[8,3,2,16,128]{4,3,2,1,0:T(8,128)}), f32[8,3,2,16,128]{4,3,2,1,0:T(8,128)S(1)}, u32[]{:S(2)}, u32[]{:S(2)}) async-start(f32[8,3,2,16,128]{4,3,2,1,0:T(8,128)} %stack.63), calls=%async_computation.8 | async-start | bytes 786432 | tf_op jit(solution)/shard_map/all_to_all | solution.py:58
  227.8 5.1 %all-to-all-done.8 = f32[8,3,2,16,128]{4,3,2,1,0:T(8,128)S(1)} async-done(((f32[8,3,2,16,128]{4,3,2,1,0:T(8,128)}), f32[8,3,2,16,128]{4,3,2,1,0:T(8,128)S(1)}, u32[]{:S(2)}, u32[]{:S(2)}) %all-to-all-start.8) | async-done | bytes 393248 | tf_op jit(solution)/shard_map/all_to_all | solution.py:58
  237.0 4.4 %collective-permute-done.35 = f32[3,18,1,128]{3,2,1,0:T(1,128)S(1)} collective-permute-done((f32[3,18,1,128]{3,2,1,0:T(1,128)S(1)}, f32[3,18,1,128]{3,2,1,0:T(1,128)S(1)}, u32[]{:S(2)}, u32[]{:S(2)}) %collective-permute-start.35) | collective-permute-done | bytes 27680 | tf_op jit(solution)/shard_map/ppermute | solution.py:26
  241.7 5.3 %collective-permute-start.37 = (f32[1,1,16,128]{3,2,1,0:T(8,128)S(1)}, f32[1,1,16,128]{3,2,1,0:T(8,128)S(1)}, u32[]{:S(2)}, u32[]{:S(2)}) collective-permute-start(f32[1,1,16,128]{3,2,1,0:T(8,128)S(1)} %get-tuple-element.118), channel_id=1, source_target_pairs={{0,120},{8,0},{16,8},{24,16},{32,24},{40,32},{48,40},{56,48},{64,5... | collective-permute-start | bytes 24584 | tf_op jit(solution)/shard_map/ppermute | solution.py:15
  248.5 9.1 %all_to_all.74 = f32[8,1,2,16,128]{4,3,2,1,0:T(8,128)S(1)} all-to-all(f32[8,1,2,16,128]{4,3,2,1,0:T(8,128)S(1)} %stack.64), channel_id=1, replica_groups=mesh['gx'=16,'gy'=8] {'gy'}, dimensions={0} | all-to-all | bytes 262144 | tf_op jit(solution)/shard_map/all_to_all | solution.py:58
  261.6 4.4 %collective-permute-done.39 = f32[1,18,1,128]{3,2,1,0:T(1,128)S(1)} collective-permute-done((f32[1,18,1,128]{3,2,1,0:T(1,128)S(1)}, f32[1,18,1,128]{3,2,1,0:T(1,128)S(1)}, u32[]{:S(2)}, u32[]{:S(2)}) %collective-permute-start.39) | collective-permute-done | bytes 9248 | tf_op jit(solution)/shard_map/ppermute | solution.py:26
  266.5 5.3 %collective-permute-start.41 = (f32[1,1,16,128]{3,2,1,0:T(8,128)S(1)}, f32[1,1,16,128]{3,2,1,0:T(8,128)S(1)}, u32[]{:S(2)}, u32[]{:S(2)}) collective-permute-start(f32[1,1,16,128]{3,2,1,0:T(8,128)S(1)} %get-tuple-element.116), channel_id=1, source_target_pairs={{0,120},{8,0},{16,8},{24,16},{32,24},{40,32},{48,40},{56,48},{64,5... | collective-permute-start | bytes 24584 | tf_op jit(solution)/shard_map/ppermute | solution.py:15
  273.3 9.1 %all_to_all.75 = f32[8,1,2,16,128]{4,3,2,1,0:T(8,128)S(1)} all-to-all(f32[8,1,2,16,128]{4,3,2,1,0:T(8,128)S(1)} %stack.65), channel_id=1, replica_groups=mesh['gx'=16,'gy'=8] {'gy'}, dimensions={0} | all-to-all | bytes 262144 | tf_op jit(solution)/shard_map/all_to_all | solution.py:58
  286.6 4.4 %collective-permute-done.43 = f32[1,18,1,128]{3,2,1,0:T(1,128)S(1)} collective-permute-done((f32[1,18,1,128]{3,2,1,0:T(1,128)S(1)}, f32[1,18,1,128]{3,2,1,0:T(1,128)S(1)}, u32[]{:S(2)}, u32[]{:S(2)}) %collective-permute-start.43) | collective-permute-done | bytes 9248 | tf_op jit(solution)/shard_map/ppermute | solution.py:26
  291.5 5.3 %collective-permute-start.45 = (f32[1,1,16,128]{3,2,1,0:T(8,128)S(1)}, f32[1,1,16,128]{3,2,1,0:T(8,128)S(1)}, u32[]{:S(2)}, u32[]{:S(2)}) collective-permute-start(f32[1,1,16,128]{3,2,1,0:T(8,128)S(1)} %get-tuple-element.114), channel_id=1, source_target_pairs={{0,120},{8,0},{16,8},{24,16},{32,24},{40,32},{48,40},{56,48},{64,5... | collective-permute-start | bytes 24584 | tf_op jit(solution)/shard_map/ppermute | solution.py:15
  298.2 9.1 %all_to_all.76 = f32[8,1,2,16,128]{4,3,2,1,0:T(8,128)S(1)} all-to-all(f32[8,1,2,16,128]{4,3,2,1,0:T(8,128)S(1)} %stack.66), channel_id=1, replica_groups=mesh['gx'=16,'gy'=8] {'gy'}, dimensions={0} | all-to-all | bytes 262144 | tf_op jit(solution)/shard_map/all_to_all | solution.py:58
  311.4 4.4 %collective-permute-done.47 = f32[1,18,1,128]{3,2,1,0:T(1,128)S(1)} collective-permute-done((f32[1,18,1,128]{3,2,1,0:T(1,128)S(1)}, f32[1,18,1,128]{3,2,1,0:T(1,128)S(1)}, u32[]{:S(2)}, u32[]{:S(2)}) %collective-permute-start.47) | collective-permute-done | bytes 9248 | tf_op jit(solution)/shard_map/ppermute | solution.py:26
  316.3 5.3 %collective-permute-start.49 = (f32[1,1,16,128]{3,2,1,0:T(8,128)S(1)}, f32[1,1,16,128]{3,2,1,0:T(8,128)S(1)}, u32[]{:S(2)}, u32[]{:S(2)}) collective-permute-start(f32[1,1,16,128]{3,2,1,0:T(8,128)S(1)} %get-tuple-element.112), channel_id=1, source_target_pairs={{0,120},{8,0},{16,8},{24,16},{32,24},{40,32},{48,40},{56,48},{64,5... | collective-permute-start | bytes 24584 | tf_op jit(solution)/shard_map/ppermute | solution.py:15
  323.0 9.1 %all_to_all.77 = f32[8,1,2,16,128]{4,3,2,1,0:T(8,128)S(1)} all-to-all(f32[8,1,2,16,128]{4,3,2,1,0:T(8,128)S(1)} %stack.67), channel_id=1, replica_groups=mesh['gx'=16,'gy'=8] {'gy'}, dimensions={0} | all-to-all | bytes 262144 | tf_op jit(solution)/shard_map/all_to_all | solution.py:58
  336.2 4.4 %collective-permute-done.51 = f32[1,18,1,128]{3,2,1,0:T(1,128)S(1)} collective-permute-done((f32[1,18,1,128]{3,2,1,0:T(1,128)S(1)}, f32[1,18,1,128]{3,2,1,0:T(1,128)S(1)}, u32[]{:S(2)}, u32[]{:S(2)}) %collective-permute-start.51) | collective-permute-done | bytes 9248 | tf_op jit(solution)/shard_map/ppermute | solution.py:26
  341.1 5.3 %collective-permute-start.53 = (f32[1,1,16,128]{3,2,1,0:T(8,128)S(1)}, f32[1,1,16,128]{3,2,1,0:T(8,128)S(1)}, u32[]{:S(2)}, u32[]{:S(2)}) collective-permute-start(f32[1,1,16,128]{3,2,1,0:T(8,128)S(1)} %get-tuple-element.106), channel_id=1, source_target_pairs={{0,120},{8,0},{16,8},{24,16},{32,24},{40,32},{48,40},{56,48},{64,5... | collective-permute-start | bytes 24584 | tf_op jit(solution)/shard_map/ppermute | solution.py:15
  348.4 5.4 %all-to-all-start.13 = ((f32[8,1,2,16,128]{4,3,2,1,0:T(8,128)}), f32[8,1,2,16,128]{4,3,2,1,0:T(8,128)S(1)}, u32[]{:S(2)}, u32[]{:S(2)}) async-start(f32[8,1,2,16,128]{4,3,2,1,0:T(8,128)} %stack.68), calls=%async_computation.13 | async-start | bytes 262144 | tf_op jit(solution)/shard_map/all_to_all | solution.py:58
  354.0 3.8 %all-to-all-done.13 = f32[8,1,2,16,128]{4,3,2,1,0:T(8,128)S(1)} async-done(((f32[8,1,2,16,128]{4,3,2,1,0:T(8,128)}), f32[8,1,2,16,128]{4,3,2,1,0:T(8,128)S(1)}, u32[]{:S(2)}, u32[]{:S(2)}) %all-to-all-start.13) | async-done | bytes 131104 | tf_op jit(solution)/shard_map/all_to_all | solution.py:58
  361.8 4.4 %collective-permute-done.55 = f32[1,18,1,128]{3,2,1,0:T(1,128)S(1)} collective-permute-done((f32[1,18,1,128]{3,2,1,0:T(1,128)S(1)}, f32[1,18,1,128]{3,2,1,0:T(1,128)S(1)}, u32[]{:S(2)}, u32[]{:S(2)}) %collective-permute-start.55) | collective-permute-done | bytes 9248 | tf_op jit(solution)/shard_map/ppermute | solution.py:26
  (265 shorter events, 89.1 us)
Async XLA Ops:
  0.8 8.0 %collective-permute-start = (f32[4,1,16,128]{3,2,1,0:T(8,128)S(1)}, f32[4,1,16,128]{3,2,1,0:T(8,128)S(1)}, u32[]{:S(2)}, u32[]{:S(2)}) collective-permute-start(f32[4,1,16,128]{3,2,1,0:T(8,128)S(1)} %get-tuple-element.39), channel_id=1, source_target_pairs={{0,8},{8,16},{16,24},{24,32},{32,40},{40,48},{48,56},{56,64},{64,7... | collective-permute-start | bytes 98312 | tf_op jit(solution)/shard_map/ppermute | solution.py:15
  0.8 8.0 %collective-permute-start.1 = (f32[4,1,16,128]{3,2,1,0:T(8,128)S(1)}, f32[4,1,16,128]{3,2,1,0:T(8,128)S(1)}, u32[]{:S(2)}, u32[]{:S(2)}) collective-permute-start(f32[4,1,16,128]{3,2,1,0:T(8,128)S(1)} %get-tuple-element.40), channel_id=1, source_target_pairs={{0,120},{8,0},{16,8},{24,16},{32,24},{40,32},{48,40},{56,48},{64,5... | collective-permute-start | bytes 98312 | tf_op jit(solution)/shard_map/ppermute | solution.py:15
  9.6 12.7 %all-to-all-start = ((f32[8,4,2,16,128]{4,3,2,1,0:T(8,128)}), f32[8,4,2,16,128]{4,3,2,1,0:T(8,128)S(1)}, u32[]{:S(2)}, u32[]{:S(2)}) async-start(f32[8,4,2,16,128]{4,3,2,1,0:T(8,128)} %stack.48), calls=%async_computation | async-start | bytes 1048576 | tf_op jit(solution)/shard_map/all_to_all | solution.py:58
  22.5 6.1 %collective-permute-start.2 = (f32[4,18,1,128]{3,2,1,0:T(1,128)S(1)}, f32[4,18,1,128]{3,2,1,0:T(1,128)S(1)}, u32[]{:S(2)}, u32[]{:S(2)}) collective-permute-start(f32[4,18,1,128]{3,2,1,0:T(1,128)S(1)} %get-tuple-element.19), channel_id=1, source_target_pairs={{1,0},{2,1},{3,2},{4,3},{5,4},{6,5},{7,6},{0,7},{9,8},{10,9},{11,1... | collective-permute-start | bytes 110600 | tf_op jit(solution)/shard_map/ppermute | solution.py:26
  29.3 6.9 %collective-permute-start.4 = (f32[3,1,16,128]{3,2,1,0:T(8,128)S(1)}, f32[3,1,16,128]{3,2,1,0:T(8,128)S(1)}, u32[]{:S(2)}, u32[]{:S(2)}) collective-permute-start(f32[3,1,16,128]{3,2,1,0:T(8,128)S(1)} %get-tuple-element.32), channel_id=1, source_target_pairs={{0,8},{8,16},{16,24},{24,32},{32,40},{40,48},{48,56},{56,64},{64,7... | collective-permute-start | bytes 73736 | tf_op jit(solution)/shard_map/ppermute | solution.py:15
  29.4 6.9 %collective-permute-start.5 = (f32[3,1,16,128]{3,2,1,0:T(8,128)S(1)}, f32[3,1,16,128]{3,2,1,0:T(8,128)S(1)}, u32[]{:S(2)}, u32[]{:S(2)}) collective-permute-start(f32[3,1,16,128]{3,2,1,0:T(8,128)S(1)} %get-tuple-element.33), channel_id=1, source_target_pairs={{0,120},{8,0},{16,8},{24,16},{32,24},{40,32},{48,40},{56,48},{64,5... | collective-permute-start | bytes 73736 | tf_op jit(solution)/shard_map/ppermute | solution.py:15
  37.0 13.9 %all-to-all-start.1 = ((f32[8,3,2,16,128]{4,3,2,1,0:T(8,128)}), f32[8,3,2,16,128]{4,3,2,1,0:T(8,128)S(1)}, u32[]{:S(2)}, u32[]{:S(2)}) async-start(f32[8,3,2,16,128]{4,3,2,1,0:T(8,128)} %stack.50), calls=%async_computation.1 | async-start | bytes 786432 | tf_op jit(solution)/shard_map/all_to_all | solution.py:58
  53.4 6.0 %collective-permute-start.7 = (f32[3,18,1,128]{3,2,1,0:T(1,128)S(1)}, f32[3,18,1,128]{3,2,1,0:T(1,128)S(1)}, u32[]{:S(2)}, u32[]{:S(2)}) collective-permute-start(f32[3,18,1,128]{3,2,1,0:T(1,128)S(1)} %get-tuple-element.52), channel_id=1, source_target_pairs={{1,0},{2,1},{3,2},{4,3},{5,4},{6,5},{7,6},{0,7},{9,8},{10,9},{11,1... | collective-permute-start | bytes 82952 | tf_op jit(solution)/shard_map/ppermute | solution.py:26
  59.6 6.8 %collective-permute-start.8 = (f32[1,1,16,128]{3,2,1,0:T(8,128)S(1)}, f32[1,1,16,128]{3,2,1,0:T(8,128)S(1)}, u32[]{:S(2)}, u32[]{:S(2)}) collective-permute-start(f32[1,1,16,128]{3,2,1,0:T(8,128)S(1)} %get-tuple-element.137), channel_id=1, source_target_pairs={{0,8},{8,16},{16,24},{24,32},{32,40},{40,48},{48,56},{56,64},{64,7... | collective-permute-start | bytes 24584 | tf_op jit(solution)/shard_map/ppermute | solution.py:15
  59.6 6.7 %collective-permute-start.9 = (f32[1,1,16,128]{3,2,1,0:T(8,128)S(1)}, f32[1,1,16,128]{3,2,1,0:T(8,128)S(1)}, u32[]{:S(2)}, u32[]{:S(2)}) collective-permute-start(f32[1,1,16,128]{3,2,1,0:T(8,128)S(1)} %get-tuple-element.138), channel_id=1, source_target_pairs={{0,120},{8,0},{16,8},{24,16},{32,24},{40,32},{48,40},{56,48},{64,5... | collective-permute-start | bytes 24584 | tf_op jit(solution)/shard_map/ppermute | solution.py:15
  78.1 5.8 %collective-permute-start.11 = (f32[1,18,1,128]{3,2,1,0:T(1,128)S(1)}, f32[1,18,1,128]{3,2,1,0:T(1,128)S(1)}, u32[]{:S(2)}, u32[]{:S(2)}) collective-permute-start(f32[1,18,1,128]{3,2,1,0:T(1,128)S(1)} %get-tuple-element.104), channel_id=1, source_target_pairs={{1,0},{2,1},{3,2},{4,3},{5,4},{6,5},{7,6},{0,7},{9,8},{10,9},{11,1... | collective-permute-start | bytes 27656 | tf_op jit(solution)/shard_map/ppermute | solution.py:26
  84.3 6.8 %collective-permute-start.12 = (f32[1,1,16,128]{3,2,1,0:T(8,128)S(1)}, f32[1,1,16,128]{3,2,1,0:T(8,128)S(1)}, u32[]{:S(2)}, u32[]{:S(2)}) collective-permute-start(f32[1,1,16,128]{3,2,1,0:T(8,128)S(1)} %get-tuple-element.135), channel_id=1, source_target_pairs={{0,8},{8,16},{16,24},{24,32},{32,40},{40,48},{48,56},{56,64},{64,7... | collective-permute-start | bytes 24584 | tf_op jit(solution)/shard_map/ppermute | solution.py:15
  84.4 6.7 %collective-permute-start.13 = (f32[1,1,16,128]{3,2,1,0:T(8,128)S(1)}, f32[1,1,16,128]{3,2,1,0:T(8,128)S(1)}, u32[]{:S(2)}, u32[]{:S(2)}) collective-permute-start(f32[1,1,16,128]{3,2,1,0:T(8,128)S(1)} %get-tuple-element.136), channel_id=1, source_target_pairs={{0,120},{8,0},{16,8},{24,16},{32,24},{40,32},{48,40},{56,48},{64,5... | collective-permute-start | bytes 24584 | tf_op jit(solution)/shard_map/ppermute | solution.py:15
  102.9 5.8 %collective-permute-start.15 = (f32[1,18,1,128]{3,2,1,0:T(1,128)S(1)}, f32[1,18,1,128]{3,2,1,0:T(1,128)S(1)}, u32[]{:S(2)}, u32[]{:S(2)}) collective-permute-start(f32[1,18,1,128]{3,2,1,0:T(1,128)S(1)} %get-tuple-element.102), channel_id=1, source_target_pairs={{1,0},{2,1},{3,2},{4,3},{5,4},{6,5},{7,6},{0,7},{9,8},{10,9},{11,1... | collective-permute-start | bytes 27656 | tf_op jit(solution)/shard_map/ppermute | solution.py:26
  109.1 6.8 %collective-permute-start.16 = (f32[1,1,16,128]{3,2,1,0:T(8,128)S(1)}, f32[1,1,16,128]{3,2,1,0:T(8,128)S(1)}, u32[]{:S(2)}, u32[]{:S(2)}) collective-permute-start(f32[1,1,16,128]{3,2,1,0:T(8,128)S(1)} %get-tuple-element.133), channel_id=1, source_target_pairs={{0,8},{8,16},{16,24},{24,32},{32,40},{40,48},{48,56},{56,64},{64,7... | collective-permute-start | bytes 24584 | tf_op jit(solution)/shard_map/ppermute | solution.py:15
  109.2 6.7 %collective-permute-start.17 = (f32[1,1,16,128]{3,2,1,0:T(8,128)S(1)}, f32[1,1,16,128]{3,2,1,0:T(8,128)S(1)}, u32[]{:S(2)}, u32[]{:S(2)}) collective-permute-start(f32[1,1,16,128]{3,2,1,0:T(8,128)S(1)} %get-tuple-element.134), channel_id=1, source_target_pairs={{0,120},{8,0},{16,8},{24,16},{32,24},{40,32},{48,40},{56,48},{64,5... | collective-permute-start | bytes 24584 | tf_op jit(solution)/shard_map/ppermute | solution.py:15
  127.7 5.8 %collective-permute-start.19 = (f32[1,18,1,128]{3,2,1,0:T(1,128)S(1)}, f32[1,18,1,128]{3,2,1,0:T(1,128)S(1)}, u32[]{:S(2)}, u32[]{:S(2)}) collective-permute-start(f32[1,18,1,128]{3,2,1,0:T(1,128)S(1)} %get-tuple-element.100), channel_id=1, source_target_pairs={{1,0},{2,1},{3,2},{4,3},{5,4},{6,5},{7,6},{0,7},{9,8},{10,9},{11,1... | collective-permute-start | bytes 27656 | tf_op jit(solution)/shard_map/ppermute | solution.py:26
  133.9 6.8 %collective-permute-start.20 = (f32[1,1,16,128]{3,2,1,0:T(8,128)S(1)}, f32[1,1,16,128]{3,2,1,0:T(8,128)S(1)}, u32[]{:S(2)}, u32[]{:S(2)}) collective-permute-start(f32[1,1,16,128]{3,2,1,0:T(8,128)S(1)} %get-tuple-element.131), channel_id=1, source_target_pairs={{0,8},{8,16},{16,24},{24,32},{32,40},{40,48},{48,56},{56,64},{64,7... | collective-permute-start | bytes 24584 | tf_op jit(solution)/shard_map/ppermute | solution.py:15
  133.9 6.7 %collective-permute-start.21 = (f32[1,1,16,128]{3,2,1,0:T(8,128)S(1)}, f32[1,1,16,128]{3,2,1,0:T(8,128)S(1)}, u32[]{:S(2)}, u32[]{:S(2)}) collective-permute-start(f32[1,1,16,128]{3,2,1,0:T(8,128)S(1)} %get-tuple-element.132), channel_id=1, source_target_pairs={{0,120},{8,0},{16,8},{24,16},{32,24},{40,32},{48,40},{56,48},{64,5... | collective-permute-start | bytes 24584 | tf_op jit(solution)/shard_map/ppermute | solution.py:15
  152.4 5.8 %collective-permute-start.23 = (f32[1,18,1,128]{3,2,1,0:T(1,128)S(1)}, f32[1,18,1,128]{3,2,1,0:T(1,128)S(1)}, u32[]{:S(2)}, u32[]{:S(2)}) collective-permute-start(f32[1,18,1,128]{3,2,1,0:T(1,128)S(1)} %get-tuple-element.98), channel_id=1, source_target_pairs={{1,0},{2,1},{3,2},{4,3},{5,4},{6,5},{7,6},{0,7},{9,8},{10,9},{11,1... | collective-permute-start | bytes 27656 | tf_op jit(solution)/shard_map/ppermute | solution.py:26
  158.6 6.8 %collective-permute-start.24 = (f32[1,1,16,128]{3,2,1,0:T(8,128)S(1)}, f32[1,1,16,128]{3,2,1,0:T(8,128)S(1)}, u32[]{:S(2)}, u32[]{:S(2)}) collective-permute-start(f32[1,1,16,128]{3,2,1,0:T(8,128)S(1)} %get-tuple-element.129), channel_id=1, source_target_pairs={{0,8},{8,16},{16,24},{24,32},{32,40},{40,48},{48,56},{56,64},{64,7... | collective-permute-start | bytes 24584 | tf_op jit(solution)/shard_map/ppermute | solution.py:15
  158.7 6.7 %collective-permute-start.25 = (f32[1,1,16,128]{3,2,1,0:T(8,128)S(1)}, f32[1,1,16,128]{3,2,1,0:T(8,128)S(1)}, u32[]{:S(2)}, u32[]{:S(2)}) collective-permute-start(f32[1,1,16,128]{3,2,1,0:T(8,128)S(1)} %get-tuple-element.130), channel_id=1, source_target_pairs={{0,120},{8,0},{16,8},{24,16},{32,24},{40,32},{48,40},{56,48},{64,5... | collective-permute-start | bytes 24584 | tf_op jit(solution)/shard_map/ppermute | solution.py:15
  166.1 9.3 %all-to-all-start.6 = ((f32[8,1,2,16,128]{4,3,2,1,0:T(8,128)}), f32[8,1,2,16,128]{4,3,2,1,0:T(8,128)S(1)}, u32[]{:S(2)}, u32[]{:S(2)}) async-start(f32[8,1,2,16,128]{4,3,2,1,0:T(8,128)} %stack.55), calls=%async_computation.6 | async-start | bytes 262144 | tf_op jit(solution)/shard_map/all_to_all | solution.py:58
  178.1 5.8 %collective-permute-start.27 = (f32[1,18,1,128]{3,2,1,0:T(1,128)S(1)}, f32[1,18,1,128]{3,2,1,0:T(1,128)S(1)}, u32[]{:S(2)}, u32[]{:S(2)}) collective-permute-start(f32[1,18,1,128]{3,2,1,0:T(1,128)S(1)} %get-tuple-element.96), channel_id=1, source_target_pairs={{1,0},{2,1},{3,2},{4,3},{5,4},{6,5},{7,6},{0,7},{9,8},{10,9},{11,1... | collective-permute-start | bytes 27656 | tf_op jit(solution)/shard_map/ppermute | solution.py:26
  184.7 7.0 %collective-permute-start.28 = (f32[4,1,16,128]{3,2,1,0:T(8,128)S(1)}, f32[4,1,16,128]{3,2,1,0:T(8,128)S(1)}, u32[]{:S(2)}, u32[]{:S(2)}) collective-permute-start(f32[4,1,16,128]{3,2,1,0:T(8,128)S(1)} %get-tuple-element.25), channel_id=1, source_target_pairs={{0,8},{8,16},{16,24},{24,32},{32,40},{40,48},{48,56},{56,64},{64,7... | collective-permute-start | bytes 98312 | tf_op jit(solution)/shard_map/ppermute | solution.py:15
  184.8 6.9 %collective-permute-start.29 = (f32[4,1,16,128]{3,2,1,0:T(8,128)S(1)}, f32[4,1,16,128]{3,2,1,0:T(8,128)S(1)}, u32[]{:S(2)}, u32[]{:S(2)}) collective-permute-start(f32[4,1,16,128]{3,2,1,0:T(8,128)S(1)} %get-tuple-element.26), channel_id=1, source_target_pairs={{0,120},{8,0},{16,8},{24,16},{32,24},{40,32},{48,40},{56,48},{64,5... | collective-permute-start | bytes 98312 | tf_op jit(solution)/shard_map/ppermute | solution.py:15
  193.2 11.4 %all-to-all-start.7 = ((f32[8,4,2,16,128]{4,3,2,1,0:T(8,128)}), f32[8,4,2,16,128]{4,3,2,1,0:T(8,128)S(1)}, u32[]{:S(2)}, u32[]{:S(2)}) async-start(f32[8,4,2,16,128]{4,3,2,1,0:T(8,128)} %stack.59), calls=%async_computation.7 | async-start | bytes 1048576 | tf_op jit(solution)/shard_map/all_to_all | solution.py:58
  205.5 6.1 %collective-permute-start.30 = (f32[4,18,1,128]{3,2,1,0:T(1,128)S(1)}, f32[4,18,1,128]{3,2,1,0:T(1,128)S(1)}, u32[]{:S(2)}, u32[]{:S(2)}) collective-permute-start(f32[4,18,1,128]{3,2,1,0:T(1,128)S(1)} %get-tuple-element.17), channel_id=1, source_target_pairs={{1,0},{2,1},{3,2},{4,3},{5,4},{6,5},{7,6},{0,7},{9,8},{10,9},{11,1... | collective-permute-start | bytes 110600 | tf_op jit(solution)/shard_map/ppermute | solution.py:26
  212.3 6.9 %collective-permute-start.32 = (f32[3,1,16,128]{3,2,1,0:T(8,128)S(1)}, f32[3,1,16,128]{3,2,1,0:T(8,128)S(1)}, u32[]{:S(2)}, u32[]{:S(2)}) collective-permute-start(f32[3,1,16,128]{3,2,1,0:T(8,128)S(1)} %get-tuple-element.23), channel_id=1, source_target_pairs={{0,8},{8,16},{16,24},{24,32},{32,40},{40,48},{48,56},{56,64},{64,7... | collective-permute-start | bytes 73736 | tf_op jit(solution)/shard_map/ppermute | solution.py:15
  212.4 6.9 %collective-permute-start.33 = (f32[3,1,16,128]{3,2,1,0:T(8,128)S(1)}, f32[3,1,16,128]{3,2,1,0:T(8,128)S(1)}, u32[]{:S(2)}, u32[]{:S(2)}) collective-permute-start(f32[3,1,16,128]{3,2,1,0:T(8,128)S(1)} %get-tuple-element.24), channel_id=1, source_target_pairs={{0,120},{8,0},{16,8},{24,16},{32,24},{40,32},{48,40},{56,48},{64,5... | collective-permute-start | bytes 73736 | tf_op jit(solution)/shard_map/ppermute | solution.py:15
  220.1 12.9 %all-to-all-start.8 = ((f32[8,3,2,16,128]{4,3,2,1,0:T(8,128)}), f32[8,3,2,16,128]{4,3,2,1,0:T(8,128)S(1)}, u32[]{:S(2)}, u32[]{:S(2)}) async-start(f32[8,3,2,16,128]{4,3,2,1,0:T(8,128)} %stack.63), calls=%async_computation.8 | async-start | bytes 786432 | tf_op jit(solution)/shard_map/all_to_all | solution.py:58
  235.5 6.0 %collective-permute-start.35 = (f32[3,18,1,128]{3,2,1,0:T(1,128)S(1)}, f32[3,18,1,128]{3,2,1,0:T(1,128)S(1)}, u32[]{:S(2)}, u32[]{:S(2)}) collective-permute-start(f32[3,18,1,128]{3,2,1,0:T(1,128)S(1)} %get-tuple-element.50), channel_id=1, source_target_pairs={{1,0},{2,1},{3,2},{4,3},{5,4},{6,5},{7,6},{0,7},{9,8},{10,9},{11,1... | collective-permute-start | bytes 82952 | tf_op jit(solution)/shard_map/ppermute | solution.py:26
  241.7 6.8 %collective-permute-start.36 = (f32[1,1,16,128]{3,2,1,0:T(8,128)S(1)}, f32[1,1,16,128]{3,2,1,0:T(8,128)S(1)}, u32[]{:S(2)}, u32[]{:S(2)}) collective-permute-start(f32[1,1,16,128]{3,2,1,0:T(8,128)S(1)} %get-tuple-element.117), channel_id=1, source_target_pairs={{0,8},{8,16},{16,24},{24,32},{32,40},{40,48},{48,56},{56,64},{64,7... | collective-permute-start | bytes 24584 | tf_op jit(solution)/shard_map/ppermute | solution.py:15
  241.7 6.7 %collective-permute-start.37 = (f32[1,1,16,128]{3,2,1,0:T(8,128)S(1)}, f32[1,1,16,128]{3,2,1,0:T(8,128)S(1)}, u32[]{:S(2)}, u32[]{:S(2)}) collective-permute-start(f32[1,1,16,128]{3,2,1,0:T(8,128)S(1)} %get-tuple-element.118), channel_id=1, source_target_pairs={{0,120},{8,0},{16,8},{24,16},{32,24},{40,32},{48,40},{56,48},{64,5... | collective-permute-start | bytes 24584 | tf_op jit(solution)/shard_map/ppermute | solution.py:15
  260.3 5.8 %collective-permute-start.39 = (f32[1,18,1,128]{3,2,1,0:T(1,128)S(1)}, f32[1,18,1,128]{3,2,1,0:T(1,128)S(1)}, u32[]{:S(2)}, u32[]{:S(2)}) collective-permute-start(f32[1,18,1,128]{3,2,1,0:T(1,128)S(1)} %get-tuple-element.94), channel_id=1, source_target_pairs={{1,0},{2,1},{3,2},{4,3},{5,4},{6,5},{7,6},{0,7},{9,8},{10,9},{11,1... | collective-permute-start | bytes 27656 | tf_op jit(solution)/shard_map/ppermute | solution.py:26
  266.4 6.8 %collective-permute-start.40 = (f32[1,1,16,128]{3,2,1,0:T(8,128)S(1)}, f32[1,1,16,128]{3,2,1,0:T(8,128)S(1)}, u32[]{:S(2)}, u32[]{:S(2)}) collective-permute-start(f32[1,1,16,128]{3,2,1,0:T(8,128)S(1)} %get-tuple-element.115), channel_id=1, source_target_pairs={{0,8},{8,16},{16,24},{24,32},{32,40},{40,48},{48,56},{56,64},{64,7... | collective-permute-start | bytes 24584 | tf_op jit(solution)/shard_map/ppermute | solution.py:15
  266.5 6.7 %collective-permute-start.41 = (f32[1,1,16,128]{3,2,1,0:T(8,128)S(1)}, f32[1,1,16,128]{3,2,1,0:T(8,128)S(1)}, u32[]{:S(2)}, u32[]{:S(2)}) collective-permute-start(f32[1,1,16,128]{3,2,1,0:T(8,128)S(1)} %get-tuple-element.116), channel_id=1, source_target_pairs={{0,120},{8,0},{16,8},{24,16},{32,24},{40,32},{48,40},{56,48},{64,5... | collective-permute-start | bytes 24584 | tf_op jit(solution)/shard_map/ppermute | solution.py:15
  285.2 5.8 %collective-permute-start.43 = (f32[1,18,1,128]{3,2,1,0:T(1,128)S(1)}, f32[1,18,1,128]{3,2,1,0:T(1,128)S(1)}, u32[]{:S(2)}, u32[]{:S(2)}) collective-permute-start(f32[1,18,1,128]{3,2,1,0:T(1,128)S(1)} %get-tuple-element.92), channel_id=1, source_target_pairs={{1,0},{2,1},{3,2},{4,3},{5,4},{6,5},{7,6},{0,7},{9,8},{10,9},{11,1... | collective-permute-start | bytes 27656 | tf_op jit(solution)/shard_map/ppermute | solution.py:26
  291.4 6.8 %collective-permute-start.44 = (f32[1,1,16,128]{3,2,1,0:T(8,128)S(1)}, f32[1,1,16,128]{3,2,1,0:T(8,128)S(1)}, u32[]{:S(2)}, u32[]{:S(2)}) collective-permute-start(f32[1,1,16,128]{3,2,1,0:T(8,128)S(1)} %get-tuple-element.113), channel_id=1, source_target_pairs={{0,8},{8,16},{16,24},{24,32},{32,40},{40,48},{48,56},{56,64},{64,7... | collective-permute-start | bytes 24584 | tf_op jit(solution)/shard_map/ppermute | solution.py:15
  291.5 6.7 %collective-permute-start.45 = (f32[1,1,16,128]{3,2,1,0:T(8,128)S(1)}, f32[1,1,16,128]{3,2,1,0:T(8,128)S(1)}, u32[]{:S(2)}, u32[]{:S(2)}) collective-permute-start(f32[1,1,16,128]{3,2,1,0:T(8,128)S(1)} %get-tuple-element.114), channel_id=1, source_target_pairs={{0,120},{8,0},{16,8},{24,16},{32,24},{40,32},{48,40},{56,48},{64,5... | collective-permute-start | bytes 24584 | tf_op jit(solution)/shard_map/ppermute | solution.py:15
  310.0 5.8 %collective-permute-start.47 = (f32[1,18,1,128]{3,2,1,0:T(1,128)S(1)}, f32[1,18,1,128]{3,2,1,0:T(1,128)S(1)}, u32[]{:S(2)}, u32[]{:S(2)}) collective-permute-start(f32[1,18,1,128]{3,2,1,0:T(1,128)S(1)} %get-tuple-element.90), channel_id=1, source_target_pairs={{1,0},{2,1},{3,2},{4,3},{5,4},{6,5},{7,6},{0,7},{9,8},{10,9},{11,1... | collective-permute-start | bytes 27656 | tf_op jit(solution)/shard_map/ppermute | solution.py:26
  316.2 6.8 %collective-permute-start.48 = (f32[1,1,16,128]{3,2,1,0:T(8,128)S(1)}, f32[1,1,16,128]{3,2,1,0:T(8,128)S(1)}, u32[]{:S(2)}, u32[]{:S(2)}) collective-permute-start(f32[1,1,16,128]{3,2,1,0:T(8,128)S(1)} %get-tuple-element.111), channel_id=1, source_target_pairs={{0,8},{8,16},{16,24},{24,32},{32,40},{40,48},{48,56},{56,64},{64,7... | collective-permute-start | bytes 24584 | tf_op jit(solution)/shard_map/ppermute | solution.py:15
  316.3 6.7 %collective-permute-start.49 = (f32[1,1,16,128]{3,2,1,0:T(8,128)S(1)}, f32[1,1,16,128]{3,2,1,0:T(8,128)S(1)}, u32[]{:S(2)}, u32[]{:S(2)}) collective-permute-start(f32[1,1,16,128]{3,2,1,0:T(8,128)S(1)} %get-tuple-element.112), channel_id=1, source_target_pairs={{0,120},{8,0},{16,8},{24,16},{32,24},{40,32},{48,40},{56,48},{64,5... | collective-permute-start | bytes 24584 | tf_op jit(solution)/shard_map/ppermute | solution.py:15
  334.8 5.8 %collective-permute-start.51 = (f32[1,18,1,128]{3,2,1,0:T(1,128)S(1)}, f32[1,18,1,128]{3,2,1,0:T(1,128)S(1)}, u32[]{:S(2)}, u32[]{:S(2)}) collective-permute-start(f32[1,18,1,128]{3,2,1,0:T(1,128)S(1)} %get-tuple-element.88), channel_id=1, source_target_pairs={{1,0},{2,1},{3,2},{4,3},{5,4},{6,5},{7,6},{0,7},{9,8},{10,9},{11,1... | collective-permute-start | bytes 27656 | tf_op jit(solution)/shard_map/ppermute | solution.py:26
  341.0 6.8 %collective-permute-start.52 = (f32[1,1,16,128]{3,2,1,0:T(8,128)S(1)}, f32[1,1,16,128]{3,2,1,0:T(8,128)S(1)}, u32[]{:S(2)}, u32[]{:S(2)}) collective-permute-start(f32[1,1,16,128]{3,2,1,0:T(8,128)S(1)} %get-tuple-element.105), channel_id=1, source_target_pairs={{0,8},{8,16},{16,24},{24,32},{32,40},{40,48},{48,56},{56,64},{64,7... | collective-permute-start | bytes 24584 | tf_op jit(solution)/shard_map/ppermute | solution.py:15
  341.1 6.7 %collective-permute-start.53 = (f32[1,1,16,128]{3,2,1,0:T(8,128)S(1)}, f32[1,1,16,128]{3,2,1,0:T(8,128)S(1)}, u32[]{:S(2)}, u32[]{:S(2)}) collective-permute-start(f32[1,1,16,128]{3,2,1,0:T(8,128)S(1)} %get-tuple-element.106), channel_id=1, source_target_pairs={{0,120},{8,0},{16,8},{24,16},{32,24},{40,32},{48,40},{56,48},{64,5... | collective-permute-start | bytes 24584 | tf_op jit(solution)/shard_map/ppermute | solution.py:15
  348.4 9.3 %all-to-all-start.13 = ((f32[8,1,2,16,128]{4,3,2,1,0:T(8,128)}), f32[8,1,2,16,128]{4,3,2,1,0:T(8,128)S(1)}, u32[]{:S(2)}, u32[]{:S(2)}) async-start(f32[8,1,2,16,128]{4,3,2,1,0:T(8,128)} %stack.68), calls=%async_computation.13 | async-start | bytes 262144 | tf_op jit(solution)/shard_map/all_to_all | solution.py:58
  360.4 5.8 %collective-permute-start.55 = (f32[1,18,1,128]{3,2,1,0:T(1,128)S(1)}, f32[1,18,1,128]{3,2,1,0:T(1,128)S(1)}, u32[]{:S(2)}, u32[]{:S(2)}) collective-permute-start(f32[1,18,1,128]{3,2,1,0:T(1,128)S(1)} %get-tuple-element.86), channel_id=1, source_target_pairs={{1,0},{2,1},{3,2},{4,3},{5,4},{6,5},{7,6},{0,7},{9,8},{10,9},{11,1... | collective-permute-start | bytes 27656 | tf_op jit(solution)/shard_map/ppermute | solution.py:26
  (22 other events, 78.2 us)
